TPU v7x, 128 devices: a whole 4x4x4 slice. The times are simulated.
128 devices in a mesh: dp: 8 (over z, core), mp: 16 (over x, y).
Axes of the slice: x: 4, y: 4, z: 4, core: 2. Of those that a mesh axis runs over, the one named last changes fastest.
Arguments:
- gradient: bfloat16 [100663296], P(('dp', 'mp'))
- block_position: int32 [96], replicated, may hold values from 0 to 95, as said below
- block_owner: int32 [96], replicated, may hold values from 0 to 127, as said below
- left_stats: float32 [128, 1024, 1024], P(('dp', 'mp'))
- right_stats: float32 [128, 1024, 1024], P(('dp', 'mp'))
- left_root: bfloat16 [128, 1024, 1024], P(('dp', 'mp'))
- right_root: bfloat16 [128, 1024, 1024], P(('dp', 'mp'))
Outputs:
- update: bfloat16 [100663296], P(('dp', 'mp'))
- new_left: float32 [128, 1024, 1024], P(('dp', 'mp'))
- new_right: float32 [128, 1024, 1024], P(('dp', 'mp'))
Inputs may be any that keep to these rules, and one draw needn't show every extreme that they name: `block_position`: a permutation of the block numbers. `block_owner`: all owners differ; the owner of the block at position p is one of the devices 4 * (p // 3) to 4 * (p // 3) + 3; devices 0 and 128 - 1 always own a block.
All inputs are finite; a program needn't handle non-finite values.
Results may differ from a plain program's by a relative error of at most 0.0057.
Values may be sent and summed in bfloat16 or wider, within the bound.
A program may use at most 128 MiB of HBM per device.

v0:
```python
import jax
import jax.numpy as jnp
from jax import lax
from jax.sharding import PartitionSpec as P

DECAY_RATE = 0.95
EPSILON = 1e-06


def from_behind(block, axis, distance):
    devices = range(lax.axis_size(axis))
    route = [(i - distance, i) for i in devices if i - distance in devices]
    return lax.ppermute(block, axis, route)


def local(gradient, block_position, block_owner, left_stats, right_stats, left_root, right_root):
    block_size = left_stats.shape[1]
    rows_held = gradient.shape[0] // block_size
    grad_rows = gradient.reshape(rows_held, block_size)
    myself = lax.axis_index("dp") * lax.axis_size("mp") + lax.axis_index("mp")

    def holding(device):
        owned = block_owner == device
        return (jnp.any(owned), jnp.sum(jnp.where(owned, block_position, 0)))

    owns_block, my_place = holding(myself)
    grad_total = lax.psum(jnp.sum(jnp.square(grad_rows.astype(jnp.float32))), ("dp", "mp"))
    slabs = []
    for offset in range(-3, 4):
        if offset == 0:
            slabs.append(grad_rows)
        else:
            slabs.append(from_behind(grad_rows, ("dp", "mp"), -offset))
    window = jnp.concatenate(slabs, axis=0)
    first_device = myself - 3
    first_row = my_place * block_size - first_device * rows_held
    first_row = jnp.clip(first_row, 0, window.shape[0] - block_size)
    taken = lax.dynamic_slice_in_dim(window, first_row, block_size, 0)
    grad_block = jnp.where(owns_block, taken, jnp.zeros_like(taken))
    gram_left = jnp.dot(grad_block, grad_block.T, preferred_element_type=jnp.float32)
    gram_right = jnp.dot(grad_block.T, grad_block, preferred_element_type=jnp.float32)
    new_left = DECAY_RATE * left_stats[0] + (1.0 - DECAY_RATE) / block_size * gram_left
    new_right = DECAY_RATE * right_stats[0] + (1.0 - DECAY_RATE) / block_size * gram_right
    left_half = jnp.dot(left_root[0], grad_block, preferred_element_type=jnp.float32).astype(
        jnp.bfloat16
    )
    direction = jnp.dot(left_half, right_root[0], preferred_element_type=jnp.float32).astype(
        jnp.bfloat16
    )
    direction_local = jnp.sum(jnp.square(direction.astype(jnp.float32)))
    direction_total = lax.psum(direction_local, ("dp", "mp"))
    graft_scale = jnp.sqrt(grad_total / (direction_total + EPSILON))
    outgoing = (graft_scale * direction.astype(jnp.float32)).astype(jnp.bfloat16)

    def placed(matrix, source):
        source_owns, source_place = holding(source)
        padded = jnp.pad(matrix, ((rows_held, rows_held), (0, 0)))
        first_slab = myself * rows_held - source_place * block_size + rows_held
        correlation = source_owns & (first_slab >= 0) & (first_slab <= block_size + rows_held)
        slab_rows = lax.dynamic_slice_in_dim(
            padded, jnp.clip(first_slab, 0, block_size + rows_held), rows_held, 0
        )
        return jnp.where(correlation, slab_rows, jnp.zeros_like(slab_rows))

    returned = placed(outgoing, myself)
    for offset in range(-3, 4):
        if offset != 0:
            arrived = from_behind(outgoing, ("dp", "mp"), -offset)
            returned = returned + placed(arrived, myself + offset)
    return (returned.reshape(-1), new_left[None], new_right[None])


def solution(mesh):
    placed = (
        P(("dp", "mp")),
        P(),
        P(),
        P(("dp", "mp"), None, None),
        P(("dp", "mp"), None, None),
        P(("dp", "mp"), None, None),
        P(("dp", "mp"), None, None),
    )
    return jax.shard_map(
        local,
        mesh=mesh,
        in_specs=placed,
        out_specs=(P(("dp", "mp")), P(("dp", "mp"), None, None), P(("dp", "mp"), None, None)),
        check_vma=False,
    )
```

profile of v0, /device:TPU:0, one launch (start us, length us, event | category | flops | bytes accessed | tf_op | source)
XLA Modules:
  0.0 513.8 jit_solution(16165085102969159678)
XLA Ops:
  0.7 3.8 reshape.16
  4.5 6.2 %collective-permute-start = (bf16[768,1024]{1,0:T(8,128)(2,1)}, bf16[768,1024]{1,0:T(8,128)(2,1)}, u32[]{:S(2)}, u32[]{:S(2)}) collective-permute-start(bf16[768,1024]{1,0:T(8,128)(2,1)} %reshape.16), channel_id=1, source_target_pairs={{0,3},{1,4},{2,5},{3,6},{4,7},{5,8},{6,9},{7,10},{8,11},{9,12},{10... | collective-permute-start | bytes 4718600 | tf_op jit(solution)/shard_map/ppermute | solution.py:13
  10.7 4.7 collective-permute-start.1
  15.3 2.9 collective-permute-start.2
  20.8 123.8 %collective-permute-done = bf16[768,1024]{1,0:T(8,128)(2,1)} collective-permute-done((bf16[768,1024]{1,0:T(8,128)(2,1)}, bf16[768,1024]{1,0:T(8,128)(2,1)}, u32[]{:S(2)}, u32[]{:S(2)}) %collective-permute-start) | collective-permute-done | bytes 1572896 | tf_op jit(solution)/shard_map/ppermute | solution.py:13
  148.1 2.9 multiply_reduce_fusion
  151.0 2.7 constant_dynamic-update-slice_fusion.6
  153.7 2.8 constant_dynamic-update-slice_fusion.5
  160.4 2.7 constant_dynamic-update-slice_fusion.2
  163.1 2.8 constant_dynamic-update-slice_fusion.1
  165.9 18.1 %collective-permute-done.5 = bf16[768,1024]{1,0:T(8,128)(2,1)} collective-permute-done((bf16[768,1024]{1,0:T(8,128)(2,1)}, bf16[768,1024]{1,0:T(8,128)(2,1)}, u32[]{:S(2)}, u32[]{:S(2)}) %collective-permute-start.5) | collective-permute-done | bytes 1572896 | tf_op jit(solution)/shard_map/ppermute | solution.py:13
  184.0 2.7 constant_dynamic-update-slice_fusion
  186.7 9.5 %fusion = (f32[]{:T(128)}, bf16[1024,1024]{1,0:T(8,128)(2,1)}) fusion(bf16[1,1024,1024]{2,1,0:T(8,128)(2,1)S(1)} %copy-done, bf16[1,1024,1024]{2,1,0:T(8,128)(2,1)} %param.12, bf16[5376,1024]{1,0:T(8,128)(2,1)} %constant_dynamic-update-slice_fusion, s32[]{:T(128)S(6)} %min.25, pred[]{:T(512)} %get-tuple-element.14), kind=kOutput, calls=%fused_computation.9 | convolution fusion | flops 4301258752 | bytes 8389128 | tf_op jit(solution)/shard_map/dot_general | solution.py:47
  196.2 67.3 %all-reduce.7 = (f32[]{:T(128)}, f32[]{:T(128)}) all-reduce(f32[]{:T(128)} %multiply_reduce_fusion, f32[]{:T(128)} %get-tuple-element.19), channel_id=1, replica_groups=mesh['dp'=8,'mp'=16] {'dp','mp'}, use_global_device_ids=true, to_apply=%region_3.4 | all-reduce | flops 2 | bytes 16 | tf_op jit(solution)/shard_map/psum | solution.py:27
  264.9 3.5 fusion.1
  270.9 8.6 %collective-permute-start.6 = (bf16[1024,1024]{1,0:T(8,128)(2,1)}, bf16[1024,1024]{1,0:T(8,128)(2,1)}, u32[]{:S(2)}, u32[]{:S(2)}) collective-permute-start(bf16[1024,1024]{1,0:T(8,128)(2,1)} %fusion.1), channel_id=1, source_target_pairs={{0,3},{1,4},{2,5},{3,6},{4,7},{5,8},{6,9},{7,10},{8,11},{9,12},{10... | collective-permute-start | bytes 6291464 | tf_op jit(solution)/shard_map/ppermute | solution.py:13
  279.5 5.9 %collective-permute-start.7 = (bf16[1024,1024]{1,0:T(8,128)(2,1)}, bf16[1024,1024]{1,0:T(8,128)(2,1)}, u32[]{:S(2)}, u32[]{:S(2)}) collective-permute-start(bf16[1024,1024]{1,0:T(8,128)(2,1)} %fusion.1), channel_id=1, source_target_pairs={{0,2},{1,3},{2,4},{3,5},{4,6},{5,7},{6,8},{7,9},{8,10},{9,11},{10,... | collective-permute-start | bytes 6291464 | tf_op jit(solution)/shard_map/ppermute | solution.py:13
  285.4 3.0 collective-permute-start.8
  288.4 166.9 %collective-permute-done.10 = bf16[1024,1024]{1,0:T(8,128)(2,1)} collective-permute-done((bf16[1024,1024]{1,0:T(8,128)(2,1)}, bf16[1024,1024]{1,0:T(8,128)(2,1)}, u32[]{:S(2)}, u32[]{:S(2)}) %collective-permute-start.10) | collective-permute-done | bytes 2097184 | tf_op jit(solution)/shard_map/ppermute | solution.py:13
  464.8 9.2 %fusion.2 = f32[1,1024,1024]{2,1,0:T(8,128)} fusion(f32[1,1024,1024]{2,1,0:T(8,128)} %param.11, bf16[5376,1024]{1,0:T(8,128)(2,1)} %constant_dynamic-update-slice_fusion, s32[]{:T(128)S(6)} %min.25, pred[]{:T(512)} %get-tuple-element.14), kind=kOutput, calls=%fused_computation.12 | convolution fusion | flops 2151677952 | bytes 10486276 | tf_op jit(solution)/shard_map/dot_general | solution.py:41
  474.0 7.5 %fusion.3 = f32[1,1024,1024]{2,1,0:T(8,128)} fusion(f32[1,1024,1024]{2,1,0:T(8,128)S(1)} %copy-done.4, bf16[5376,1024]{1,0:T(8,128)(2,1)} %constant_dynamic-update-slice_fusion, s32[]{:T(128)S(6)} %min.25, pred[]{:T(512)} %get-tuple-element.14), kind=kOutput, calls=%fused_computation.14 | convolution fusion | flops 2151677952 | bytes 10486276 | tf_op jit(solution)/shard_map/dot_general | solution.py:40
  481.5 14.8 %collective-permute-done.8 = bf16[1024,1024]{1,0:T(8,128)(2,1)} collective-permute-done((bf16[1024,1024]{1,0:T(8,128)(2,1)}, bf16[1024,1024]{1,0:T(8,128)(2,1)}, u32[]{:S(2)}, u32[]{:S(2)}) %collective-permute-start.8) | collective-permute-done | bytes 2097184 | tf_op jit(solution)/shard_map/ppermute | solution.py:13
  496.3 6.9 %collective-permute-done.9 = bf16[1024,1024]{1,0:T(8,128)(2,1)} collective-permute-done((bf16[1024,1024]{1,0:T(8,128)(2,1)}, bf16[1024,1024]{1,0:T(8,128)(2,1)}, u32[]{:S(2)}, u32[]{:S(2)}) %collective-permute-start.9) | collective-permute-done | bytes 2097184 | tf_op jit(solution)/shard_map/ppermute | solution.py:13
  503.1 9.1 %fusion.27 = bf16[96,8,8,128]{3,2,1,0:T(8,128)(2,1)S(1)} fusion(s32[]{:T(128)S(6)} %min.32, bf16[1024,1024]{1,0:T(8,128)(2,1)} %collective-permute-done.11, pred[]{:T(512)S(6)} %and.57, s32[]{:T(128)S(6)} %min.31, bf16[1024,1024]{1,0:T(8,128)(2,1)} %collective-permute-done.10, pred[]{:T(512)S(6)} %and.55, s32[]{:T(128)S(6)} %min.30, ...), kind=kLoop, calls=%fused_computation.36 | loop fusion | flops 16515072 | bytes 16252963
  (28 shorter events, 15.0 us)
Async XLA Ops:
  0.6 186.1 %copy-start = (bf16[1,1024,1024]{2,1,0:T(8,128)(2,1)S(1)}, bf16[1,1024,1024]{2,1,0:T(8,128)(2,1)}, u32[]{:S(2)}) copy-start(bf16[1,1024,1024]{2,1,0:T(8,128)(2,1)} %param.13) | copy-start | bytes 6291460
  0.6 145.2 %copy-start.3 = (s32[96]{0:T(128)S(1)}, s32[96]{0:T(128)}, u32[]{:S(2)}) copy-start(s32[96]{0:T(128)} %param.8) | copy-start | bytes 1156
  0.7 145.2 %copy-start.2 = (s32[96]{0:T(128)S(1)}, s32[96]{0:T(128)}, u32[]{:S(2)}) copy-start(s32[96]{0:T(128)} %param.9) | copy-start | bytes 1156
  4.5 140.1 %collective-permute-start = (bf16[768,1024]{1,0:T(8,128)(2,1)}, bf16[768,1024]{1,0:T(8,128)(2,1)}, u32[]{:S(2)}, u32[]{:S(2)}) collective-permute-start(bf16[768,1024]{1,0:T(8,128)(2,1)} %reshape.16), channel_id=1, source_target_pairs={{0,3},{1,4},{2,5},{3,6},{4,7},{5,8},{6,9},{7,10},{8,11},{9,12},{10... | collective-permute-start | bytes 4718600 | tf_op jit(solution)/shard_map/ppermute | solution.py:13
  10.7 143.0 %collective-permute-start.1 = (bf16[768,1024]{1,0:T(8,128)(2,1)}, bf16[768,1024]{1,0:T(8,128)(2,1)}, u32[]{:S(2)}, u32[]{:S(2)}) collective-permute-start(bf16[768,1024]{1,0:T(8,128)(2,1)} %reshape.16), channel_id=1, source_target_pairs={{0,2},{1,3},{2,4},{3,5},{4,6},{5,7},{6,8},{7,9},{8,10},{9,11},{10,... | collective-permute-start | bytes 4718600 | tf_op jit(solution)/shard_map/ppermute | solution.py:13
  15.3 141.2 %collective-permute-start.2 = (bf16[768,1024]{1,0:T(8,128)(2,1)}, bf16[768,1024]{1,0:T(8,128)(2,1)}, u32[]{:S(2)}, u32[]{:S(2)}) collective-permute-start(bf16[768,1024]{1,0:T(8,128)(2,1)} %reshape.16), channel_id=1, source_target_pairs={{0,1},{1,2},{2,3},{3,4},{4,5},{5,6},{6,7},{7,8},{8,9},{9,10},{10,1... | collective-permute-start | bytes 4718600 | tf_op jit(solution)/shard_map/ppermute | solution.py:13
  18.2 142.2 %collective-permute-start.3 = (bf16[768,1024]{1,0:T(8,128)(2,1)}, bf16[768,1024]{1,0:T(8,128)(2,1)}, u32[]{:S(2)}, u32[]{:S(2)}) collective-permute-start(bf16[768,1024]{1,0:T(8,128)(2,1)} %reshape.16), channel_id=1, source_target_pairs={{1,0},{2,1},{3,2},{4,3},{5,4},{6,5},{7,6},{8,7},{9,8},{10,9},{11,1... | collective-permute-start | bytes 4718600 | tf_op jit(solution)/shard_map/ppermute | solution.py:13
  19.5 143.6 %collective-permute-start.4 = (bf16[768,1024]{1,0:T(8,128)(2,1)}, bf16[768,1024]{1,0:T(8,128)(2,1)}, u32[]{:S(2)}, u32[]{:S(2)}) collective-permute-start(bf16[768,1024]{1,0:T(8,128)(2,1)} %reshape.16), channel_id=1, source_target_pairs={{2,0},{3,1},{4,2},{5,3},{6,4},{7,5},{8,6},{9,7},{10,8},{11,9},{12,... | collective-permute-start | bytes 4718600 | tf_op jit(solution)/shard_map/ppermute | solution.py:13
  144.6 39.4 %collective-permute-start.5 = (bf16[768,1024]{1,0:T(8,128)(2,1)}, bf16[768,1024]{1,0:T(8,128)(2,1)}, u32[]{:S(2)}, u32[]{:S(2)}) collective-permute-start(bf16[768,1024]{1,0:T(8,128)(2,1)} %reshape.16), channel_id=1, source_target_pairs={{3,0},{4,1},{5,2},{6,3},{7,4},{8,5},{9,6},{10,7},{11,8},{12,9},{13... | collective-permute-start | bytes 4718600 | tf_op jit(solution)/shard_map/ppermute | solution.py:13
  153.7 5.5 %copy-start.1 = (bf16[768,1024]{1,0:T(8,128)(2,1)S(1)}, bf16[768,1024]{1,0:T(8,128)(2,1)}, u32[]{:S(2)}) copy-start(bf16[768,1024]{1,0:T(8,128)(2,1)} %reshape.16) | copy-start | bytes 4718596
  268.3 187.0 %collective-permute-start.10 = (bf16[1024,1024]{1,0:T(8,128)(2,1)}, bf16[1024,1024]{1,0:T(8,128)(2,1)}, u32[]{:S(2)}, u32[]{:S(2)}) collective-permute-start(bf16[1024,1024]{1,0:T(8,128)(2,1)} %fusion.1), channel_id=1, source_target_pairs={{2,0},{3,1},{4,2},{5,3},{6,4},{7,5},{8,6},{9,7},{10,8},{11,9},{12,... | collective-permute-start | bytes 6291464 | tf_op jit(solution)/shard_map/ppermute | solution.py:13
  269.6 211.9 %collective-permute-start.11 = (bf16[1024,1024]{1,0:T(8,128)(2,1)}, bf16[1024,1024]{1,0:T(8,128)(2,1)}, u32[]{:S(2)}, u32[]{:S(2)}) collective-permute-start(bf16[1024,1024]{1,0:T(8,128)(2,1)} %fusion.1), channel_id=1, source_target_pairs={{3,0},{4,1},{5,2},{6,3},{7,4},{8,5},{9,6},{10,7},{11,8},{12,9},{13... | collective-permute-start | bytes 6291464 | tf_op jit(solution)/shard_map/ppermute | solution.py:13
  270.9 210.6 %collective-permute-start.6 = (bf16[1024,1024]{1,0:T(8,128)(2,1)}, bf16[1024,1024]{1,0:T(8,128)(2,1)}, u32[]{:S(2)}, u32[]{:S(2)}) collective-permute-start(bf16[1024,1024]{1,0:T(8,128)(2,1)} %fusion.1), channel_id=1, source_target_pairs={{0,3},{1,4},{2,5},{3,6},{4,7},{5,8},{6,9},{7,10},{8,11},{9,12},{10... | collective-permute-start | bytes 6291464 | tf_op jit(solution)/shard_map/ppermute | solution.py:13
  279.5 202.0 %collective-permute-start.7 = (bf16[1024,1024]{1,0:T(8,128)(2,1)}, bf16[1024,1024]{1,0:T(8,128)(2,1)}, u32[]{:S(2)}, u32[]{:S(2)}) collective-permute-start(bf16[1024,1024]{1,0:T(8,128)(2,1)} %fusion.1), channel_id=1, source_target_pairs={{0,2},{1,3},{2,4},{3,5},{4,6},{5,7},{6,8},{7,9},{8,10},{9,11},{10,... | collective-permute-start | bytes 6291464 | tf_op jit(solution)/shard_map/ppermute | solution.py:13
  285.4 210.9 %collective-permute-start.8 = (bf16[1024,1024]{1,0:T(8,128)(2,1)}, bf16[1024,1024]{1,0:T(8,128)(2,1)}, u32[]{:S(2)}, u32[]{:S(2)}) collective-permute-start(bf16[1024,1024]{1,0:T(8,128)(2,1)} %fusion.1), channel_id=1, source_target_pairs={{0,1},{1,2},{2,3},{3,4},{4,5},{5,6},{6,7},{7,8},{8,9},{9,10},{10,1... | collective-permute-start | bytes 6291464 | tf_op jit(solution)/shard_map/ppermute | solution.py:13
  455.3 47.8 %collective-permute-start.9 = (bf16[1024,1024]{1,0:T(8,128)(2,1)}, bf16[1024,1024]{1,0:T(8,128)(2,1)}, u32[]{:S(2)}, u32[]{:S(2)}) collective-permute-start(bf16[1024,1024]{1,0:T(8,128)(2,1)} %fusion.1), channel_id=1, source_target_pairs={{1,0},{2,1},{3,2},{4,3},{5,4},{6,5},{7,6},{8,7},{9,8},{10,9},{11,1... | collective-permute-start | bytes 6291464 | tf_op jit(solution)/shard_map/ppermute | solution.py:13
  464.8 9.2 %copy-start.4 = (f32[1,1024,1024]{2,1,0:T(8,128)S(1)}, f32[1,1024,1024]{2,1,0:T(8,128)}, u32[]{:S(2)}) copy-start(f32[1,1024,1024]{2,1,0:T(8,128)} %param.10) | copy-start | bytes 12582916
where the time goes:
time: 515 us; the launch traced here: 514 us
  waiting for transfers between devices  330 us (64%)
  blocking collectives  67.3 us (13%)
  starting transfers between devices  39.1 us (8%)
  matrix products  26.2 us (5%)
  local copies, waits for them, and re-layouts  23 us (4%)
  other arithmetic  17 us (3%)
  between operations  10.9 us (2%)
    ppermute x12, waiting for transfers between devices, from_behind(): return lax.ppermute(block, axis, route)  330 us
    psum x1, blocking collectives, local(): lax.psum(jnp.sum(jnp.square(grad_rows.astype(jnp.float32))), ('dp', 'mp'))  67.3 us
    ppermute x12, starting transfers between devices, from_behind(): return lax.ppermute(block, axis, route)  39.1 us
    unnamed x17, local copies, waits for them, and re-layouts  16.5 us
  transfers between devices with their start and end apart: 12, of which 5 were waited for; matrix products, arithmetic and copies ran while one was open for 7% of the time, Pallas kernels for 0%

commit v1 on v0

v1 whole, which is shorter than its diff:
```python
import functools
import itertools

import jax
import jax.numpy as jnp
import numpy as np
from jax import lax
from jax.experimental import pallas as pl
from jax.experimental.pallas import tpu as pltpu
from jax.sharding import PartitionSpec as P

DECAY_RATE = 0.95
EPSILON = 1e-06
MESH = pl.DeviceIdType.MESH

RING = 4
GROUP_BLOCKS = 3
B = 1024
PIECE = 128
HELD = 6
OWNED = B // PIECE
COLS = 256
QUARTERS = B // COLS
SLOTS = 6
EARLY = 3
EARLIER = B - COLS
WORDS = 8
LANES = 128
SUBROWS = B // LANES
F32, BF16 = jnp.float32, jnp.bfloat16


def schedule(wanted):
    ways = (1, RING - 1)
    far = [i for i in range(RING) if wanted[i][(i + 2) % RING]]
    best = None
    for split in itertools.product(*[range(len(wanted[i][(i + 2) % RING]) + 1) for i in far]):
        plus = dict(zip(far, split))
        first = {}
        for i in range(RING):
            pieces = wanted[i][(i + 2) % RING]
            n = plus.get(i, 0)
            first[i, 0], first[i, 1] = pieces[:n], pieces[n:]
        if max(len(p) for p in first.values()) > EARLY:
            continue
        loads = [
            len(first[i, w]) + len(first[(i - way) % RING, w]) + len(wanted[i][(i + way) % RING])
            for i in range(RING)
            for w, way in enumerate(ways)
        ]
        key = (max(loads), sum(v * v for v in loads))
        if best is None or key < best[0]:
            best = (key, first)
    assert best is not None and best[0][0] <= SLOTS
    first = best[1]
    sent = {}
    for i in range(RING):
        for w, way in enumerate(ways):
            slots = [None] * SLOTS
            for k, piece in enumerate(first[i, w]):
                slots[k] = ("own", piece)
            for k, piece in enumerate(first[(i - way) % RING, w]):
                slots[EARLY + k] = ("pass", piece)
            free = [t for t in range(SLOTS) if slots[t] is None]
            for t, piece in zip(free, wanted[i][(i + way) % RING]):
                slots[t] = ("own", piece)
            sent[i, w] = slots
    return sent


def packed(codes):
    return sum(int(c) << (5 * k) for k, c in enumerate(codes))


def tables():
    out = np.zeros((RING**GROUP_BLOCKS, RING, WORDS), np.int32)
    for owners in itertools.permutations(range(RING), GROUP_BLOCKS):
        row = (owners[0] * RING + owners[1]) * RING + owners[2]
        there = [[[] for _ in range(RING)] for _ in range(RING)]
        back = [[[] for _ in range(RING)] for _ in range(RING)]
        for piece in range(RING * HELD):
            holder, owner = piece // HELD, owners[piece // OWNED]
            there[holder][owner].append(piece)
            back[owner][holder].append(piece)
        for wanted, size, word in ((there, HELD, 0), (back, OWNED, 4)):
            sent = schedule(wanted)
            for i in range(RING):
                for w in range(2):
                    codes = []
                    for entry in sent[i, w]:
                        if entry is None:
                            codes.append(0)
                        elif entry[0] == "own":
                            codes.append(entry[1] % size)
                        else:
                            codes.append(size)
                    out[row, i, word + w] = packed(codes)
                arrived = {}
                for w, way in enumerate((1, RING - 1)):
                    for t, entry in enumerate(sent[(i - way) % RING, w]):
                        if entry is not None:
                            arrived[entry[1]] = size + w * SLOTS + t
                if word == 0:
                    codes = [HELD + 2 * SLOTS] * OWNED
                    if i in owners:
                        first = owners.index(i) * OWNED
                        for q in range(OWNED):
                            piece = first + q
                            mine = piece // HELD == i
                            codes[q] = piece % HELD if mine else arrived[piece]
                    out[row, i, 2] = packed(codes[:6])
                    out[row, i, 3] = packed(codes[6:])
                else:
                    codes = []
                    for k in range(HELD):
                        piece = i * HELD + k
                        mine = owners[piece // OWNED] == i
                        codes.append(piece % OWNED if mine else arrived[piece])
                    out[row, i, 6] = packed(codes)
    return out.reshape(-1)


def code(word, k):
    return lax.bitwise_and(lax.shift_right_logical(word, jnp.int32(5 * k)), jnp.int32(31))


def kernel(
    sizes,
    position_in,
    owner_in,
    table_in,
    gradient,
    left_stats,
    right_stats,
    left_root,
    right_root,
    wide,
    scale,
    new_left,
    new_right,
    position,
    owner,
    table,
    flat,
    grads,
    left,
    right,
    half,
    begun,
    own,
    there_out,
    there_in,
    product,
    back_out,
    back_in,
    sums_out,
    sums_in,
    local_sem,
    there_send,
    there_recv,
    back_send,
    back_recv,
    sums_send,
    sums_recv,
):
    xs, ys, zs, cores = sizes
    dp, mp = lax.axis_index("dp"), lax.axis_index("mp")
    z, core = dp // cores, dp % cores
    x, y = mp // ys, mp % ys

    def at(x, y, z, core):
        return (z * cores + core, x * ys + y)

    neighbours = (at(x, (y + 1) % ys, z, core), at(x, (y + ys - 1) % ys, z, core))

    here = (x, y, z, core)
    rounds = [(place, size) for place, size in ((1, ys), (0, xs), (2, zs), (3, cores)) if size > 1]

    def along(place, size, distance):
        there = list(here)
        there[place] = (here[place] + distance) % size
        return at(*there)

    greeted = [along(place, size, d) for place, size in rounds for d in range(1, size)]

    barrier = pltpu.get_barrier_semaphore()
    for device in greeted:
        pl.semaphore_signal(barrier, inc=1, device_id=device, device_id_type=MESH)

    loads = [
        pltpu.make_async_copy(source, target, local_sem.at[k])
        for k, (source, target) in enumerate(
            (
                (gradient, flat),
                (left_root, left),
                (right_root, right),
                (left_stats, new_left),
                (right_stats, new_right),
                (position_in, position),
                (owner_in, owner),
                (table_in, table),
            )
        )
    ]
    for k in (5, 6, 7, 0, 1, 2, 3, 4):
        loads[k].start()

    group = (dp * (xs * ys) + mp) // RING

    def find(b, found):
        place, device = position[b], owner[b]
        return tuple(
            jnp.where(place == GROUP_BLOCKS * group + k, device, f) for k, f in enumerate(found)
        )

    for k in (5, 6, 7):
        loads[k].wait()
    zero = jnp.int32(0)
    found = lax.fori_loop(0, position.shape[0], find, (zero,) * GROUP_BLOCKS)
    row = zero
    for f in found:
        row = row * RING + (f - RING * group)
    row = jnp.clip(row, 0, RING**GROUP_BLOCKS - 1)
    base = (row * RING + y) * WORDS
    words = [table[base + k] for k in range(7)]

    loads[0].wait()
    grad_sum = jnp.zeros((8, LANES), F32)
    rows = PIECE * SUBROWS
    for k in range(HELD):
        values = flat[pl.ds(k * rows, rows), :].astype(F32)
        wide[pl.ds(k * rows, rows), :] = values
        grad_sum += jnp.sum(jnp.square(values).reshape(rows // 8, 8, LANES), axis=0)

    def take(s):
        for k in range(HELD):
            for h in range(COLS // LANES):
                start = k * rows + s * (COLS // LANES) + h
                block = wide[pl.ds(start, PIECE, stride=SUBROWS), :]
                own[s][k, :, h * LANES : (h + 1) * LANES] = block.astype(BF16)

    def copy_of(out, into, send, recv, s, w, late):
        slots = pl.ds(w * SLOTS + late * EARLY, EARLY)
        return pltpu.make_async_remote_copy(
            src_ref=out[s].at[slots],
            dst_ref=into[s].at[slots],
            send_sem=send.at[s],
            recv_sem=recv.at[s, 2 * late + w],
            device_id=neighbours[w],
            device_id_type=MESH,
        )

    def send_own(out, into, send, recv, source, pair, size, s):
        for w in range(2):
            for t in range(EARLY):
                out[s][w * SLOTS + t] = source[s][jnp.minimum(code(pair[w], t), size - 1)]
            copy_of(out, into, send, recv, s, w, 0).start()

    def send_on(out, into, send, recv, source, pair, size, s):
        for w in range(2):
            copy_of(out, into, send, recv, s, w, 0).wait_recv()
            for t in range(EARLY, SLOTS):
                c = code(pair[w], t)
                passed = into[s][w * SLOTS + t - EARLY]
                mine = source[s][jnp.minimum(c, size - 1)]
                out[s][w * SLOTS + t] = jnp.where(c == size, passed, mine)
            copy_of(out, into, send, recv, s, w, 1).start()

    def arrive(out, into, send, recv, s):
        for w in range(2):
            copy_of(out, into, send, recv, s, w, 1).wait_recv()

    def all_sent(out, into, send, recv, s):
        pltpu.make_async_remote_copy(
            src_ref=out[s],
            dst_ref=into[s],
            send_sem=send.at[s],
            recv_sem=recv.at[s, 0],
            device_id=neighbours[0],
            device_id_type=MESH,
        ).wait_send()

    def pick(source, into, c, size, s):
        mine = source[s][jnp.minimum(c, size - 1)]
        came = into[s][jnp.clip(c - size, 0, 2 * SLOTS - 1)]
        return jnp.where(c < size, mine, came)

    there = (there_out, there_in, there_send, there_recv)
    back = (back_out, back_in, back_send, back_recv)

    def there_own(s):
        take(s)
        send_own(*there, own, words[0:2], HELD, s)

    def there_on(s):
        send_on(*there, own, words[0:2], HELD, s)

    def multiply_left(s):
        arrive(*there, s)
        for q in range(OWNED):
            c = code(words[2 + q // 6], q % 6)
            value = pick(own, there_in, c, HELD, s)
            value = jnp.where(c < HELD + 2 * SLOTS, value, jnp.zeros_like(value))
            grads[s, pl.ds(q * PIECE, PIECE), :] = value
        if s == 0:
            loads[1].wait()

        def tile(r, carry):
            at_rows = pl.ds(pl.multiple_of(r * COLS, COLS), COLS)
            part = jnp.dot(left[at_rows, :], grads[s], preferred_element_type=F32)
            half[at_rows, s * COLS : (s + 1) * COLS] = part.astype(BF16)
            return carry

        lax.fori_loop(0, B // COLS, tile, 0)

    def begin_right():
        loads[2].wait()

        def tile(r, carry):
            at_rows = pl.ds(pl.multiple_of(r * COLS, COLS), COLS)
            begun[at_rows, :] = jnp.dot(
                half[at_rows, :EARLIER], right[:EARLIER, :COLS], preferred_element_type=F32
            )
            return carry

        lax.fori_loop(0, B // COLS, tile, 0)

    pl.semaphore_wait(barrier, len(greeted))
    there_own(0)
    there_own(1)
    there_own(2)
    there_on(0)
    there_own(3)
    there_on(1)
    multiply_left(0)
    there_on(2)
    multiply_left(1)
    there_on(3)
    multiply_left(2)
    begin_right()
    multiply_left(3)

    def multiply_right(s, total):
        def tile(r, total):
            at_rows = pl.ds(pl.multiple_of(r * COLS, COLS), COLS)
            at_cols = pl.ds(s * COLS, COLS)
            if s == 0:
                part = jnp.dot(
                    half[at_rows, EARLIER:], right[EARLIER:, at_cols], preferred_element_type=F32
                )
                part = (begun[at_rows, :] + part).astype(BF16)
            else:
                part = jnp.dot(
                    half[at_rows, :], right[:, at_cols], preferred_element_type=F32
                ).astype(BF16)
            product[s][pl.ds(r * 2, 2)] = part.reshape(2, PIECE, COLS)
            squares = jnp.square(part.astype(F32))
            squares = squares[:, :LANES] + squares[:, LANES:]
            return total + jnp.sum(squares.reshape(COLS // 8, 8, LANES), axis=0)

        return lax.fori_loop(0, B // COLS, tile, total)

    def back_own(s):
        send_own(*back, product, words[4:6], OWNED, s)

    def back_on(s):
        send_on(*back, product, words[4:6], OWNED, s)

    def finish(s):
        arrive(*back, s)
        for k in range(HELD):
            value = pick(product, back_in, code(words[6], k), OWNED, s).astype(F32)
            for h in range(COLS // LANES):
                start = k * rows + s * (COLS // LANES) + h
                wide[pl.ds(start, PIECE, stride=SUBROWS), :] = value[:, h * LANES : (h + 1) * LANES]

    def exchange(r, d):
        place, size = rounds[r]
        return pltpu.make_async_remote_copy(
            src_ref=sums_out.at[r],
            dst_ref=sums_in.at[r, here[place]],
            send_sem=sums_send.at[r],
            recv_sem=sums_recv.at[r],
            device_id=along(place, size, d),
            device_id_type=MESH,
        )

    def exchange_start(r, sums):
        place, size = rounds[r]
        sums_out[r] = sums
        for d in range(1, size):
            exchange(r, d).start()

    def exchange_all(r):
        size = rounds[r][1]
        return pltpu.make_async_remote_copy(
            src_ref=sums_in.at[r, pl.ds(0, size - 1)],
            dst_ref=sums_in.at[r, pl.ds(0, size - 1)],
            send_sem=sums_send.at[r],
            recv_sem=sums_recv.at[r],
            device_id=along(*rounds[r], 1),
            device_id_type=MESH,
        )

    def exchange_end(r):
        place, size = rounds[r]
        sums_in[r, here[place]] = sums_out[r]
        exchange_all(r).wait_recv()
        return sum((sums_in[r, k] for k in range(1, size)), sums_in[r, 0])

    def exchange_sent(r):
        exchange_all(r).wait_send()

    factor = (1.0 - DECAY_RATE) / B

    def gram_left(r):
        if r == 0:
            loads[3].wait()
        at_rows = pl.ds(r * COLS, COLS)
        gram = jnp.zeros((COLS, B), F32)
        for s in range(QUARTERS):
            gram += lax.dot_general(
                grads[s, at_rows, :], grads[s], (((1,), (1,)), ((), ())), preferred_element_type=F32
            )
        new_left[at_rows, :] = DECAY_RATE * new_left[at_rows, :] + factor * gram

    def gram_right(r):
        if r == 0:
            loads[4].wait()
        at_rows = pl.ds(r * COLS, COLS)
        turned = grads[r].T
        for s in range(QUARTERS):
            at_cols = pl.ds(s * COLS, COLS)
            gram = jnp.dot(turned, grads[s], preferred_element_type=F32)
            new_right[at_rows, at_cols] = DECAY_RATE * new_right[at_rows, at_cols] + factor * gram

    direction_sum = jnp.zeros((8, LANES), F32)
    for s in range(QUARTERS - 1):
        direction_sum = multiply_right(s, direction_sum)
        back_own(s)
    direction_sum = multiply_right(QUARTERS - 1, direction_sum)
    exchange_start(0, jnp.concatenate([grad_sum, direction_sum], axis=0))
    back_on(0)
    back_own(QUARTERS - 1)
    gram_left(0)
    gram_left(1)
    back_on(1)
    gram_left(2)
    gram_left(3)
    back_on(2)
    for r in range(len(rounds)):
        totals = exchange_end(r)
        if r + 1 < len(rounds):
            exchange_start(r + 1, totals)
        if r < 3:
            gram_right(r)
    for r in range(min(len(rounds), 3), 4):
        gram_right(r)
    grad_total = jnp.sum(totals[0:8], keepdims=True)
    direction_total = jnp.sum(totals[8:16], keepdims=True)
    scale[...] = jnp.broadcast_to(jnp.sqrt(grad_total / (direction_total + EPSILON)), (8, LANES))
    finish(0)
    back_on(3)
    finish(1)
    finish(2)
    finish(3)

    for s in range(QUARTERS):
        all_sent(*there, s)
        all_sent(*back, s)
    for r in range(len(rounds)):
        exchange_sent(r)


def store(wide, scale, left, right, update, new_left, new_right, narrow, sem):
    copies = [
        pltpu.make_async_copy(left, new_left, sem.at[0]),
        pltpu.make_async_copy(right, new_right, sem.at[1]),
    ]
    for copy in copies:
        copy.start()
    rows = PIECE * SUBROWS
    for k in range(HELD):
        part = pl.ds(k * rows, rows)
        narrow[part, :] = (scale[0:1, :] * wide[part, :]).astype(BF16)
        copies.append(pltpu.make_async_copy(narrow.at[part], update.at[part], sem.at[2 + k]))
        copies[-1].start()
    for copy in copies:
        copy.wait()


def local(sizes, gradient, block_position, block_owner, left_stats, right_stats, left_root, right_root):
    xs, ys, zs, cores = sizes
    rounds = sum(size > 1 for size in sizes)
    held_rows = HELD * PIECE * SUBROWS
    outside = pl.BlockSpec(memory_space=pltpu.HBM)
    inside = pl.BlockSpec(memory_space=pltpu.VMEM)

    def quarters(*lead):
        return [pltpu.VMEM((*lead, PIECE, COLS), BF16)] * QUARTERS

    dma = pltpu.SemaphoreType.DMA
    results = pl.pallas_call(
        functools.partial(kernel, sizes),
        out_shape=(
            pltpu.VMEM((held_rows, LANES), F32),
            pltpu.VMEM((8, LANES), F32),
            pltpu.VMEM((B, B), F32),
            pltpu.VMEM((B, B), F32),
        ),
        in_specs=[outside] * 8,
        out_specs=(inside,) * 4,
        scratch_shapes=[
            pltpu.SMEM(block_position.shape, jnp.int32),
            pltpu.SMEM(block_owner.shape, jnp.int32),
            pltpu.SMEM((RING**GROUP_BLOCKS * RING * WORDS,), jnp.int32),
            pltpu.VMEM((held_rows, LANES), BF16),
            pltpu.VMEM((QUARTERS, B, COLS), BF16),
            pltpu.VMEM((B, B), BF16),
            pltpu.VMEM((B, B), BF16),
            pltpu.VMEM((B, B), BF16),
            pltpu.VMEM((B, COLS), F32),
            quarters(HELD),
            quarters(2 * SLOTS),
            quarters(2 * SLOTS),
            quarters(OWNED),
            quarters(2 * SLOTS),
            quarters(2 * SLOTS),
            pltpu.VMEM((rounds, 16, LANES), F32),
            pltpu.VMEM((rounds, 4, 16, LANES), F32),
            dma((8,)),
            dma((QUARTERS,)),
            dma((QUARTERS, 4)),
            dma((QUARTERS,)),
            dma((QUARTERS, 4)),
            dma((rounds,)),
            dma((rounds,)),
        ],
        compiler_params=pltpu.CompilerParams(
            collective_id=0, has_side_effects=True, vmem_limit_bytes=32 * 1024 * 1024
        ),
        name="shampoo",
    )(
        *(
            pltpu.with_memory_space_constraint(value, pltpu.HBM)
            for value in (
                block_position,
                block_owner,
                jnp.asarray(tables()),
                gradient.reshape(held_rows, LANES),
                left_stats[0],
                right_stats[0],
                left_root[0],
                right_root[0],
            )
        )
    )
    update, new_left, new_right = pl.pallas_call(
        store,
        out_shape=(
            jax.ShapeDtypeStruct((held_rows, LANES), BF16),
            jax.ShapeDtypeStruct((B, B), F32),
            jax.ShapeDtypeStruct((B, B), F32),
        ),
        in_specs=[inside] * 4,
        out_specs=(outside,) * 3,
        scratch_shapes=[pltpu.VMEM((held_rows, LANES), BF16), dma((2 + HELD,))],
        compiler_params=pltpu.CompilerParams(vmem_limit_bytes=4 * 1024 * 1024),
        name="store",
    )(*(pltpu.with_memory_space_constraint(value, pltpu.VMEM) for value in results))
    return (update.reshape(-1), new_left[None], new_right[None])


def solution(mesh):
    cores = 2
    sizes = (mesh.shape["mp"] // RING, RING, mesh.shape["dp"] // cores, cores)
    split = P(("dp", "mp"))
    slots = P(("dp", "mp"), None, None)
    return jax.shard_map(
        functools.partial(local, sizes),
        mesh=mesh,
        in_specs=(split, P(), P(), slots, slots, slots, slots),
        out_specs=(split, slots, slots),
        check_vma=False,
    )
```

time: 515 us -> 83.7 us (0.16)
  waiting for transfers between devices: 330 us -> 0 us
  Pallas kernels: 0 us -> 82.9 us
  blocking collectives: 67.3 us -> 0 us
  starting transfers between devices: 39.1 us -> 0 us
  matrix products: 26.2 us -> 0 us
  local copies, waits for them, and re-layouts: 23 us -> 0 us
  other arithmetic: 17 us -> 0 us
  between operations: 10.9 us -> 0.64 us
    ppermute x12 -> x0, waiting for transfers between devices: 330 us -> none  [from_behind(): return lax.ppermute(block, axis, route)]
    pallas_call x0 -> x2, Pallas kernels: none -> 82.9 us  [the longest x1 79.1 us: local(): pl.pallas_call(functools.partial(kernel, sizes), out_shape=(pltpu.VMEM((h...]
    psum x1 -> x0, blocking collectives: 67.3 us -> none  [local(): lax.psum(jnp.sum(jnp.square(grad_rows.astype(jnp.float32))), ('dp', 'mp'))]
    ppermute x12 -> x0, starting transfers between devices: 39.1 us -> none  [from_behind(): return lax.ppermute(block, axis, route)]
    dot_general x3 -> x0, matrix products: 26.2 us -> none  [the longest x1 9.54 us: local(): jnp.dot(left_half, right_root[0], preferred_element_type=jnp.float32)]
    unnamed x17 -> x0, local copies, waits for them, and re-layouts: 16.5 us -> none
    unnamed x1 -> x0, other arithmetic: 9.06 us -> none
  transfers between devices with their start and end apart: 12 -> 0, of which waited for: 5 -> 0; matrix products, arithmetic and copies ran while one was open for 7% -> 0% of each run, Pallas kernels for 0% -> 0%
where the time goes in v1:
time: 83.7 us; the launch traced here: 83.5 us
  Pallas kernels  82.9 us (99%)
    pallas_call x1, Pallas kernels, local(): pl.pallas_call(functools.partial(kernel, sizes), out_shape=(pltpu.VMEM((h...  79.1 us
    pallas_call x1, Pallas kernels, local(): pl.pallas_call(store, out_shape=(jax.ShapeDtypeStruct((held_rows, LANES),...  3.81 us

profile of v1, /device:TPU:0, one launch (start us, length us, event | category | flops | bytes accessed | tf_op | source)
XLA Modules:
  0.0 83.5 jit_solution(16030424174161366482)
XLA Ops:
  0.6 79.1 %shampoo.1 = (f32[6144,128]{1,0:T(8,128)S(1)}, f32[8,128]{1,0:T(8,128)S(1)}, f32[1024,1024]{1,0:T(8,128)S(1)}, f32[1024,1024]{1,0:T(8,128)S(1)}) custom-call(s32[96]{0:T(128)} %position_in.1, s32[96]{0:T(128)} %owner_in.1, s32[2048]{0:T(1024)} %constant.2.clone.table_in, bf16[6144,128]{1,0:T(8,128)(2,1)} %bitcast.12, f32[1024,1024]{1,0:T(8,128)} %bitcast.8, ...), custom_call_target="tpu_custom_call" | custom-call | tf_op jit(solution)/shard_map/shampoo/pallas_call | solution.py:503
  79.7 3.8 %store.1 = (bf16[6144,128]{1,0:T(8,128)(2,1)}, f32[1024,1024]{1,0:T(8,128)}, f32[1024,1024]{1,0:T(8,128)}) custom-call(f32[6144,128]{1,0:T(8,128)S(1)} %get-tuple-element.10.wide, f32[8,128]{1,0:T(8,128)S(1)} %get-tuple-element.11.scale, f32[1024,1024]{1,0:T(8,128)S(1)} %get-tuple-element.12.left, f32[1024,1024]{1,0:T(8,128)S(1)} %get-tuple-element.13.right), custom_call_target="tpu_custom_call" | custom-call | tf_op jit(solution)/shard_map/store/pallas_call | solution.py:558

commit v2 on v1

--- a/solution.py
+++ b/solution.py
@@ -174,7 +174,7 @@
     neighbours = (at(x, (y + 1) % ys, z, core), at(x, (y + ys - 1) % ys, z, core))
 
     here = (x, y, z, core)
-    rounds = [(place, size) for place, size in ((1, ys), (0, xs), (2, zs), (3, cores)) if size > 1]
+    rounds = [(place, size) for place, size in ((1, ys), (3, cores), (0, xs), (2, zs)) if size > 1]
 
     def along(place, size, distance):
         there = list(here)
@@ -182,10 +182,6 @@
         return at(*there)
 
     greeted = [along(place, size, d) for place, size in rounds for d in range(1, size)]
-
-    barrier = pltpu.get_barrier_semaphore()
-    for device in greeted:
-        pl.semaphore_signal(barrier, inc=1, device_id=device, device_id_type=MESH)
 
     loads = [
         pltpu.make_async_copy(source, target, local_sem.at[k])
@@ -205,6 +201,10 @@
     for k in (5, 6, 7, 0, 1, 2, 3, 4):
         loads[k].start()
 
+    barrier = pltpu.get_barrier_semaphore()
+    for device in greeted:
+        pl.semaphore_signal(barrier, inc=1, device_id=device, device_id_type=MESH)
+
     group = (dp * (xs * ys) + mp) // RING
 
     def find(b, found):
@@ -311,7 +311,7 @@
             half[at_rows, s * COLS : (s + 1) * COLS] = part.astype(BF16)
             return carry
 
-        lax.fori_loop(0, B // COLS, tile, 0)
+        lax.fori_loop(0, B // COLS, tile, 0, unroll=True)
 
     def begin_right():
         loads[2].wait()
@@ -323,7 +323,7 @@
             )
             return carry
 
-        lax.fori_loop(0, B // COLS, tile, 0)
+        lax.fori_loop(0, B // COLS, tile, 0, unroll=True)
 
     pl.semaphore_wait(barrier, len(greeted))
     there_own(0)
@@ -358,7 +358,7 @@
             squares = squares[:, :LANES] + squares[:, LANES:]
             return total + jnp.sum(squares.reshape(COLS // 8, 8, LANES), axis=0)
 
-        return lax.fori_loop(0, B // COLS, tile, total)
+        return lax.fori_loop(0, B // COLS, tile, total, unroll=True)
 
     def back_own(s):
         send_own(*back, product, words[4:6], OWNED, s)
@@ -448,20 +448,25 @@
     gram_left(2)
     gram_left(3)
     back_on(2)
+    rights = [functools.partial(gram_right, k) for k in range(4)]
+    steps = [
+        rights[0:2],
+        rights[2:4] + [functools.partial(finish, 0), functools.partial(back_on, 3)],
+        [functools.partial(finish, 1)],
+    ]
     for r in range(len(rounds)):
         totals = exchange_end(r)
         if r + 1 < len(rounds):
             exchange_start(r + 1, totals)
-        if r < 3:
-            gram_right(r)
-    for r in range(min(len(rounds), 3), 4):
-        gram_right(r)
+        if r < len(steps):
+            for step in steps[r]:
+                step()
+    for r in range(len(rounds), len(steps)):
+        for step in steps[r]:
+            step()
     grad_total = jnp.sum(totals[0:8], keepdims=True)
     direction_total = jnp.sum(totals[8:16], keepdims=True)
     scale[...] = jnp.broadcast_to(jnp.sqrt(grad_total / (direction_total + EPSILON)), (8, LANES))
-    finish(0)
-    back_on(3)
-    finish(1)
     finish(2)
     finish(3)
 

time: 83.7 us -> 82.4 us (0.984)
  Pallas kernels: 82.9 us -> 81.6 us
    pallas_call x1, Pallas kernels: 79.1 us -> 77.8 us  [local(): pl.pallas_call(functools.partial(kernel, sizes), out_shape=(pltpu.VMEM((h...]
where the time goes in v2:
time: 82.4 us; the launch traced here: 82.3 us
  Pallas kernels  81.6 us (99%)
    pallas_call x1, Pallas kernels, local(): pl.pallas_call(functools.partial(kernel, sizes), out_shape=(pltpu.VMEM((h...  77.8 us
    pallas_call x1, Pallas kernels, local(): pl.pallas_call(store, out_shape=(jax.ShapeDtypeStruct((held_rows, LANES),...  3.81 us

profile of v2, /device:TPU:0, one launch (start us, length us, event | category | flops | bytes accessed | tf_op | source)
XLA Modules:
  0.0 82.3 jit_solution(1137772973531733699)
XLA Ops:
  0.6 77.8 %shampoo.1 = (f32[6144,128]{1,0:T(8,128)S(1)}, f32[8,128]{1,0:T(8,128)S(1)}, f32[1024,1024]{1,0:T(8,128)S(1)}, f32[1024,1024]{1,0:T(8,128)S(1)}) custom-call(s32[96]{0:T(128)} %position_in.1, s32[96]{0:T(128)} %owner_in.1, s32[2048]{0:T(1024)} %constant.2.clone.table_in, bf16[6144,128]{1,0:T(8,128)(2,1)} %bitcast.12, f32[1024,1024]{1,0:T(8,128)} %bitcast.8, ...), custom_call_target="tpu_custom_call" | custom-call | tf_op jit(solution)/shard_map/shampoo/pallas_call | solution.py:508
  78.5 3.8 %store.1 = (bf16[6144,128]{1,0:T(8,128)(2,1)}, f32[1024,1024]{1,0:T(8,128)}, f32[1024,1024]{1,0:T(8,128)}) custom-call(f32[6144,128]{1,0:T(8,128)S(1)} %get-tuple-element.10.wide, f32[8,128]{1,0:T(8,128)S(1)} %get-tuple-element.11.scale, f32[1024,1024]{1,0:T(8,128)S(1)} %get-tuple-element.12.left, f32[1024,1024]{1,0:T(8,128)S(1)} %get-tuple-element.13.right), custom_call_target="tpu_custom_call" | custom-call | tf_op jit(solution)/shard_map/store/pallas_call | solution.py:563

commit v3 on v2

--- a/solution.py
+++ b/solution.py
@@ -26,6 +26,7 @@
 EARLIER = B - COLS
 WORDS = 8
 LANES = 128
+HUB = 1
 SUBROWS = B // LANES
 F32, BF16 = jnp.float32, jnp.bfloat16
 
@@ -174,7 +175,7 @@
     neighbours = (at(x, (y + 1) % ys, z, core), at(x, (y + ys - 1) % ys, z, core))
 
     here = (x, y, z, core)
-    rounds = [(place, size) for place, size in ((1, ys), (3, cores), (0, xs), (2, zs)) if size > 1]
+    rounds = [(place, size) for place, size in ((1, ys), (3, cores), (0, xs)) if size > 1]
 
     def along(place, size, distance):
         there = list(here)
@@ -204,6 +205,21 @@
     barrier = pltpu.get_barrier_semaphore()
     for device in greeted:
         pl.semaphore_signal(barrier, inc=1, device_id=device, device_id_type=MESH)
+    planes = len(greeted)
+    if zs > 1:
+        planes += jnp.where(z == HUB, zs - 1, 1)
+
+        @pl.when(z == HUB)
+        def _():
+            for d in range(1, zs):
+                pl.semaphore_signal(barrier, inc=1, device_id=along(2, zs, d), device_id_type=MESH)
+
+        @pl.when(z != HUB)
+        def _():
+            pl.semaphore_signal(
+                barrier, inc=1, device_id=at(x, y, HUB, core), device_id_type=MESH
+            )
+
 
     group = (dp * (xs * ys) + mp) // RING
 
@@ -325,7 +341,7 @@
 
         lax.fori_loop(0, B // COLS, tile, 0, unroll=True)
 
-    pl.semaphore_wait(barrier, len(greeted))
+    pl.semaphore_wait(barrier, planes)
     there_own(0)
     there_own(1)
     there_own(2)
@@ -410,6 +426,58 @@
 
     def exchange_sent(r):
         exchange_all(r).wait_send()
+
+    gather, spread = len(rounds), len(rounds) + 1
+
+    def plane_copy(r, source, target, device):
+        return pltpu.make_async_remote_copy(
+            src_ref=source,
+            dst_ref=target,
+            send_sem=sums_send.at[r],
+            recv_sem=sums_recv.at[r],
+            device_id=device,
+            device_id_type=MESH,
+        )
+
+    def plane_all(r, count):
+        part = sums_in.at[r, pl.ds(0, count)]
+        return plane_copy(r, part, part, along(2, zs, 1))
+
+    def planes_gather(sums):
+        sums_out[gather] = sums
+
+        @pl.when(z != HUB)
+        def _():
+            to = sums_in.at[gather, z]
+            plane_copy(gather, sums_out.at[gather], to, at(x, y, HUB, core)).start()
+
+    def planes_spread():
+        @pl.when(z == HUB)
+        def _():
+            plane_all(gather, zs - 1).wait_recv()
+            sums_in[gather, HUB] = sums_out[gather]
+            total = sum((sums_in[gather, k] for k in range(1, zs)), sums_in[gather, 0])
+            sums_out[spread] = total
+            sums_in[spread, 0] = total
+            for d in range(1, zs):
+                to = sums_in.at[spread, 0]
+                plane_copy(spread, sums_out.at[spread], to, along(2, zs, d)).start()
+
+    def planes_end():
+        @pl.when(z != HUB)
+        def _():
+            plane_all(spread, 1).wait_recv()
+
+        return sums_in[spread, 0]
+
+    def planes_sent():
+        @pl.when(z == HUB)
+        def _():
+            plane_all(spread, zs - 1).wait_send()
+
+        @pl.when(z != HUB)
+        def _():
+            plane_all(gather, 1).wait_send()
 
     factor = (1.0 - DECAY_RATE) / B
 
@@ -452,22 +520,28 @@
     steps = [
         rights[0:2],
         rights[2:4] + [functools.partial(finish, 0), functools.partial(back_on, 3)],
-        [functools.partial(finish, 1)],
+        [],
     ]
     for r in range(len(rounds)):
         totals = exchange_end(r)
         if r + 1 < len(rounds):
             exchange_start(r + 1, totals)
-        if r < len(steps):
-            for step in steps[r]:
-                step()
+        for step in steps[r]:
+            step()
     for r in range(len(rounds), len(steps)):
         for step in steps[r]:
             step()
+    if zs > 1:
+        planes_gather(totals)
+    finish(1)
+    if zs > 1:
+        planes_spread()
+    finish(2)
+    if zs > 1:
+        totals = planes_end()
     grad_total = jnp.sum(totals[0:8], keepdims=True)
     direction_total = jnp.sum(totals[8:16], keepdims=True)
     scale[...] = jnp.broadcast_to(jnp.sqrt(grad_total / (direction_total + EPSILON)), (8, LANES))
-    finish(2)
     finish(3)
 
     for s in range(QUARTERS):
@@ -475,6 +549,8 @@
         all_sent(*back, s)
     for r in range(len(rounds)):
         exchange_sent(r)
+    if zs > 1:
+        planes_sent()
 
 
 def store(wide, scale, left, right, update, new_left, new_right, narrow, sem):
@@ -496,7 +572,7 @@
 
 def local(sizes, gradient, block_position, block_owner, left_stats, right_stats, left_root, right_root):
     xs, ys, zs, cores = sizes
-    rounds = sum(size > 1 for size in sizes)
+    rounds = sum(size > 1 for size in sizes) + 1
     held_rows = HELD * PIECE * SUBROWS
     outside = pl.BlockSpec(memory_space=pltpu.HBM)
     inside = pl.BlockSpec(memory_space=pltpu.VMEM)

time: 82.4 us -> 81.3 us (0.987)
  Pallas kernels: 81.6 us -> 80.6 us
    pallas_call x1, Pallas kernels: 77.8 us -> 76.8 us  [local(): pl.pallas_call(functools.partial(kernel, sizes), out_shape=(pltpu.VMEM((h...]
where the time goes in v3:
time: 81.3 us; the launch traced here: 81.2 us
  Pallas kernels  80.6 us (99%)
    pallas_call x1, Pallas kernels, local(): pl.pallas_call(functools.partial(kernel, sizes), out_shape=(pltpu.VMEM((h...  76.8 us
    pallas_call x1, Pallas kernels, local(): pl.pallas_call(store, out_shape=(jax.ShapeDtypeStruct((held_rows, LANES),...  3.81 us

profile of v3, /device:TPU:0, one launch (start us, length us, event | category | flops | bytes accessed | tf_op | source)
XLA Modules:
  0.0 81.2 jit_solution(10419392322643663742)
XLA Ops:
  0.6 76.8 %shampoo.1 = (f32[6144,128]{1,0:T(8,128)S(1)}, f32[8,128]{1,0:T(8,128)S(1)}, f32[1024,1024]{1,0:T(8,128)S(1)}, f32[1024,1024]{1,0:T(8,128)S(1)}) custom-call(s32[96]{0:T(128)} %position_in.1, s32[96]{0:T(128)} %owner_in.1, s32[2048]{0:T(1024)} %constant.2.clone.table_in, bf16[6144,128]{1,0:T(8,128)(2,1)} %bitcast.12, f32[1024,1024]{1,0:T(8,128)} %bitcast.8, ...), custom_call_target="tpu_custom_call" | custom-call | tf_op jit(solution)/shard_map/shampoo/pallas_call | solution.py:584
  77.4 3.8 %store.1 = (bf16[6144,128]{1,0:T(8,128)(2,1)}, f32[1024,1024]{1,0:T(8,128)}, f32[1024,1024]{1,0:T(8,128)}) custom-call(f32[6144,128]{1,0:T(8,128)S(1)} %get-tuple-element.10.wide, f32[8,128]{1,0:T(8,128)S(1)} %get-tuple-element.11.scale, f32[1024,1024]{1,0:T(8,128)S(1)} %get-tuple-element.12.left, f32[1024,1024]{1,0:T(8,128)S(1)} %get-tuple-element.13.right), custom_call_target="tpu_custom_call" | custom-call | tf_op jit(solution)/shard_map/store/pallas_call | solution.py:639

commit v4 on v3

--- a/solution.py
+++ b/solution.py
@@ -184,11 +184,12 @@
 
     greeted = [along(place, size, d) for place, size in rounds for d in range(1, size)]
 
+    rows = PIECE * SUBROWS
+    parts = [pl.ds(k * rows, rows) for k in range(HELD)]
     loads = [
         pltpu.make_async_copy(source, target, local_sem.at[k])
         for k, (source, target) in enumerate(
             (
-                (gradient, flat),
                 (left_root, left),
                 (right_root, right),
                 (left_stats, new_left),
@@ -196,10 +197,11 @@
                 (position_in, position),
                 (owner_in, owner),
                 (table_in, table),
+                *((gradient.at[part], flat.at[part]) for part in parts),
             )
         )
     ]
-    for k in (5, 6, 7, 0, 1, 2, 3, 4):
+    for k in (4, 5, 6, *range(7, 7 + HELD), 0, 1, 2, 3):
         loads[k].start()
 
     barrier = pltpu.get_barrier_semaphore()
@@ -229,7 +231,7 @@
             jnp.where(place == GROUP_BLOCKS * group + k, device, f) for k, f in enumerate(found)
         )
 
-    for k in (5, 6, 7):
+    for k in (4, 5, 6):
         loads[k].wait()
     zero = jnp.int32(0)
     found = lax.fori_loop(0, position.shape[0], find, (zero,) * GROUP_BLOCKS)
@@ -240,13 +242,9 @@
     base = (row * RING + y) * WORDS
     words = [table[base + k] for k in range(7)]
 
-    loads[0].wait()
-    grad_sum = jnp.zeros((8, LANES), F32)
-    rows = PIECE * SUBROWS
-    for k in range(HELD):
-        values = flat[pl.ds(k * rows, rows), :].astype(F32)
-        wide[pl.ds(k * rows, rows), :] = values
-        grad_sum += jnp.sum(jnp.square(values).reshape(rows // 8, 8, LANES), axis=0)
+    for k, part in enumerate(parts):
+        loads[7 + k].wait()
+        wide[part, :] = flat[part, :].astype(F32)
 
     def take(s):
         for k in range(HELD):
@@ -311,49 +309,83 @@
     def there_on(s):
         send_on(*there, own, words[0:2], HELD, s)
 
-    def multiply_left(s):
+    def assemble(s):
         arrive(*there, s)
         for q in range(OWNED):
             c = code(words[2 + q // 6], q % 6)
             value = pick(own, there_in, c, HELD, s)
             value = jnp.where(c < HELD + 2 * SLOTS, value, jnp.zeros_like(value))
             grads[s, pl.ds(q * PIECE, PIECE), :] = value
+
+    def multiply_left(s):
         if s == 0:
-            loads[1].wait()
+            loads[0].wait()
 
         def tile(r, carry):
             at_rows = pl.ds(pl.multiple_of(r * COLS, COLS), COLS)
-            part = jnp.dot(left[at_rows, :], grads[s], preferred_element_type=F32)
+            roots = left[pl.ds(r * 2, 2)].reshape(COLS, B)
+            part = jnp.dot(roots, grads[s], preferred_element_type=F32)
             half[at_rows, s * COLS : (s + 1) * COLS] = part.astype(BF16)
             return carry
 
         lax.fori_loop(0, B // COLS, tile, 0, unroll=True)
 
     def begin_right():
-        loads[2].wait()
+        loads[1].wait()
 
         def tile(r, carry):
             at_rows = pl.ds(pl.multiple_of(r * COLS, COLS), COLS)
-            begun[at_rows, :] = jnp.dot(
+            part = jnp.dot(
                 half[at_rows, :EARLIER], right[:EARLIER, :COLS], preferred_element_type=F32
             )
+            begun[pl.ds(r * 2, 2)] = part.reshape(2, PIECE, COLS)
             return carry
 
         lax.fori_loop(0, B // COLS, tile, 0, unroll=True)
+
+    def back_first():
+        last = QUARTERS - 1
+        for t in range(EARLY):
+            places = [jnp.minimum(code(words[4 + w], t), OWNED - 1) for w in range(2)]
+            roots = jnp.concatenate([left[q] for q in places], axis=0)
+            start = jnp.concatenate([begun[q] for q in places], axis=0)
+            part = jnp.dot(roots, grads[last], preferred_element_type=F32).astype(BF16)
+            part = jnp.dot(part, right[EARLIER:, :COLS], preferred_element_type=F32)
+            part = (start + part).astype(BF16)
+            for w in range(2):
+                slot = w * SLOTS + t
+                back_out[0][slot] = part[w * PIECE : (w + 1) * PIECE]
+                pltpu.make_async_remote_copy(
+                    src_ref=back_out[0].at[slot],
+                    dst_ref=back_in[0].at[slot],
+                    send_sem=back_send.at[0],
+                    recv_sem=back_recv.at[0, w],
+                    device_id=neighbours[w],
+                    device_id_type=MESH,
+                ).start()
 
     pl.semaphore_wait(barrier, planes)
     there_own(0)
     there_own(1)
     there_own(2)
+    grad_sum = jnp.zeros((8, LANES), F32)
+    for part in parts:
+        squares = jnp.square(wide[part, :])
+        grad_sum += jnp.sum(squares.reshape(rows // 8, 8, LANES), axis=0)
     there_on(0)
     there_own(3)
     there_on(1)
+    assemble(0)
     multiply_left(0)
     there_on(2)
+    assemble(1)
     multiply_left(1)
     there_on(3)
+    assemble(2)
     multiply_left(2)
     begin_right()
+    assemble(3)
+    back_first()
     multiply_left(3)
 
     def multiply_right(s, total):
@@ -364,7 +396,7 @@
                 part = jnp.dot(
                     half[at_rows, EARLIER:], right[EARLIER:, at_cols], preferred_element_type=F32
                 )
-                part = (begun[at_rows, :] + part).astype(BF16)
+                part = (begun[pl.ds(r * 2, 2)].reshape(COLS, COLS) + part).astype(BF16)
             else:
                 part = jnp.dot(
                     half[at_rows, :], right[:, at_cols], preferred_element_type=F32
@@ -483,7 +515,7 @@
 
     def gram_left(r):
         if r == 0:
-            loads[3].wait()
+            loads[2].wait()
         at_rows = pl.ds(r * COLS, COLS)
         gram = jnp.zeros((COLS, B), F32)
         for s in range(QUARTERS):
@@ -494,7 +526,7 @@
 
     def gram_right(r):
         if r == 0:
-            loads[4].wait()
+            loads[3].wait()
         at_rows = pl.ds(r * COLS, COLS)
         turned = grads[r].T
         for s in range(QUARTERS):
@@ -505,7 +537,8 @@
     direction_sum = jnp.zeros((8, LANES), F32)
     for s in range(QUARTERS - 1):
         direction_sum = multiply_right(s, direction_sum)
-        back_own(s)
+        if s > 0:
+            back_own(s)
     direction_sum = multiply_right(QUARTERS - 1, direction_sum)
     exchange_start(0, jnp.concatenate([grad_sum, direction_sum], axis=0))
     back_on(0)
@@ -597,10 +630,10 @@
             pltpu.SMEM((RING**GROUP_BLOCKS * RING * WORDS,), jnp.int32),
             pltpu.VMEM((held_rows, LANES), BF16),
             pltpu.VMEM((QUARTERS, B, COLS), BF16),
+            pltpu.VMEM((OWNED, PIECE, B), BF16),
             pltpu.VMEM((B, B), BF16),
             pltpu.VMEM((B, B), BF16),
-            pltpu.VMEM((B, B), BF16),
-            pltpu.VMEM((B, COLS), F32),
+            pltpu.VMEM((OWNED, PIECE, COLS), F32),
             quarters(HELD),
             quarters(2 * SLOTS),
             quarters(2 * SLOTS),
@@ -609,7 +642,7 @@
             quarters(2 * SLOTS),
             pltpu.VMEM((rounds, 16, LANES), F32),
             pltpu.VMEM((rounds, 4, 16, LANES), F32),
-            dma((8,)),
+            dma((7 + HELD,)),
             dma((QUARTERS,)),
             dma((QUARTERS, 4)),
             dma((QUARTERS,)),
@@ -631,7 +664,7 @@
                 gradient.reshape(held_rows, LANES),
                 left_stats[0],
                 right_stats[0],
-                left_root[0],
+                left_root[0].reshape(OWNED, PIECE, B),
                 right_root[0],
             )
         )

time: 81.3 us -> 81 us (level)
  no operation moved by 1% of the time
where the time goes in v4:
time: 81 us; the launch traced here: 80.9 us
  Pallas kernels  80.3 us (99%)
    pallas_call x1, Pallas kernels, local(): pl.pallas_call(functools.partial(kernel, sizes), out_shape=(pltpu.VMEM((h...  76.5 us
    pallas_call x1, Pallas kernels, local(): pl.pallas_call(store, out_shape=(jax.ShapeDtypeStruct((held_rows, LANES),...  3.81 us

profile of v4, /device:TPU:0, one launch (start us, length us, event | category | flops | bytes accessed | tf_op | source)
XLA Modules:
  0.0 80.9 jit_solution(1121442826568778290)
XLA Ops:
  0.6 76.5 %shampoo.1 = (f32[6144,128]{1,0:T(8,128)S(1)}, f32[8,128]{1,0:T(8,128)S(1)}, f32[1024,1024]{1,0:T(8,128)S(1)}, f32[1024,1024]{1,0:T(8,128)S(1)}) custom-call(s32[96]{0:T(128)} %position_in.1, s32[96]{0:T(128)} %owner_in.1, s32[2048]{0:T(1024)} %constant.2.clone.table_in, bf16[6144,128]{1,0:T(8,128)(2,1)} %bitcast.12, f32[1024,1024]{1,0:T(8,128)} %bitcast.8, ...), custom_call_target="tpu_custom_call" | custom-call | tf_op jit(solution)/shard_map/shampoo/pallas_call | solution.py:617
  77.1 3.8 %store.1 = (bf16[6144,128]{1,0:T(8,128)(2,1)}, f32[1024,1024]{1,0:T(8,128)}, f32[1024,1024]{1,0:T(8,128)}) custom-call(f32[6144,128]{1,0:T(8,128)S(1)} %get-tuple-element.10.wide, f32[8,128]{1,0:T(8,128)S(1)} %get-tuple-element.11.scale, f32[1024,1024]{1,0:T(8,128)S(1)} %get-tuple-element.12.left, f32[1024,1024]{1,0:T(8,128)S(1)} %get-tuple-element.13.right), custom_call_target="tpu_custom_call" | custom-call | tf_op jit(solution)/shard_map/store/pallas_call | solution.py:672

commit v5 on v4

--- a/solution.py
+++ b/solution.py
@@ -259,10 +259,21 @@
             src_ref=out[s].at[slots],
             dst_ref=into[s].at[slots],
             send_sem=send.at[s],
-            recv_sem=recv.at[s, 2 * late + w],
+            recv_sem=recv.at[s, late],
             device_id=neighbours[w],
             device_id_type=MESH,
         )
+
+    def both_came(out, into, send, recv, s, late):
+        slots = pl.ds(0, 2 * EARLY)
+        pltpu.make_async_remote_copy(
+            src_ref=out[s].at[slots],
+            dst_ref=into[s].at[slots],
+            send_sem=send.at[s],
+            recv_sem=recv.at[s, late],
+            device_id=neighbours[0],
+            device_id_type=MESH,
+        ).wait_recv()
 
     def send_own(out, into, send, recv, source, pair, size, s):
         for w in range(2):
@@ -271,8 +282,8 @@
             copy_of(out, into, send, recv, s, w, 0).start()
 
     def send_on(out, into, send, recv, source, pair, size, s):
+        both_came(out, into, send, recv, s, 0)
         for w in range(2):
-            copy_of(out, into, send, recv, s, w, 0).wait_recv()
             for t in range(EARLY, SLOTS):
                 c = code(pair[w], t)
                 passed = into[s][w * SLOTS + t - EARLY]
@@ -281,8 +292,7 @@
             copy_of(out, into, send, recv, s, w, 1).start()
 
     def arrive(out, into, send, recv, s):
-        for w in range(2):
-            copy_of(out, into, send, recv, s, w, 1).wait_recv()
+        both_came(out, into, send, recv, s, 1)
 
     def all_sent(out, into, send, recv, s):
         pltpu.make_async_remote_copy(
@@ -328,7 +338,7 @@
             half[at_rows, s * COLS : (s + 1) * COLS] = part.astype(BF16)
             return carry
 
-        lax.fori_loop(0, B // COLS, tile, 0, unroll=True)
+        lax.fori_loop(0, B // COLS, tile, 0)
 
     def begin_right():
         loads[1].wait()
@@ -341,7 +351,7 @@
             begun[pl.ds(r * 2, 2)] = part.reshape(2, PIECE, COLS)
             return carry
 
-        lax.fori_loop(0, B // COLS, tile, 0, unroll=True)
+        lax.fori_loop(0, B // COLS, tile, 0)
 
     def back_first():
         last = QUARTERS - 1
@@ -359,7 +369,7 @@
                     src_ref=back_out[0].at[slot],
                     dst_ref=back_in[0].at[slot],
                     send_sem=back_send.at[0],
-                    recv_sem=back_recv.at[0, w],
+                    recv_sem=back_recv.at[0, 0],
                     device_id=neighbours[w],
                     device_id_type=MESH,
                 ).start()
@@ -644,9 +654,9 @@
             pltpu.VMEM((rounds, 4, 16, LANES), F32),
             dma((7 + HELD,)),
             dma((QUARTERS,)),
-            dma((QUARTERS, 4)),
+            dma((QUARTERS, 2)),
             dma((QUARTERS,)),
-            dma((QUARTERS, 4)),
+            dma((QUARTERS, 2)),
             dma((rounds,)),
             dma((rounds,)),
         ],

time: 81 us -> 80.8 us (level)
  no operation moved by 1% of the time
where the time goes in v5:
time: 80.8 us; the launch traced here: 80.7 us
  Pallas kernels  80.1 us (99%)
    pallas_call x1, Pallas kernels, local(): pl.pallas_call(functools.partial(kernel, sizes), out_shape=(pltpu.VMEM((h...  76.2 us
    pallas_call x1, Pallas kernels, local(): pl.pallas_call(store, out_shape=(jax.ShapeDtypeStruct((held_rows, LANES),...  3.81 us

profile of v5, /device:TPU:0, one launch (start us, length us, event | category | flops | bytes accessed | tf_op | source)
XLA Modules:
  0.0 80.7 jit_solution(12099239499600157015)
XLA Ops:
  0.6 76.2 %shampoo.1 = (f32[6144,128]{1,0:T(8,128)S(1)}, f32[8,128]{1,0:T(8,128)S(1)}, f32[1024,1024]{1,0:T(8,128)S(1)}, f32[1024,1024]{1,0:T(8,128)S(1)}) custom-call(s32[96]{0:T(128)} %position_in.1, s32[96]{0:T(128)} %owner_in.1, s32[2048]{0:T(1024)} %constant.2.clone.table_in, bf16[6144,128]{1,0:T(8,128)(2,1)} %bitcast.12, f32[1024,1024]{1,0:T(8,128)} %bitcast.8, ...), custom_call_target="tpu_custom_call" | custom-call | tf_op jit(solution)/shard_map/shampoo/pallas_call | solution.py:627
  76.9 3.8 %store.1 = (bf16[6144,128]{1,0:T(8,128)(2,1)}, f32[1024,1024]{1,0:T(8,128)}, f32[1024,1024]{1,0:T(8,128)}) custom-call(f32[6144,128]{1,0:T(8,128)S(1)} %get-tuple-element.10.wide, f32[8,128]{1,0:T(8,128)S(1)} %get-tuple-element.11.scale, f32[1024,1024]{1,0:T(8,128)S(1)} %get-tuple-element.12.left, f32[1024,1024]{1,0:T(8,128)S(1)} %get-tuple-element.13.right), custom_call_target="tpu_custom_call" | custom-call | tf_op jit(solution)/shard_map/store/pallas_call | solution.py:682

commit v6 on v5

--- a/solution.py
+++ b/solution.py
@@ -275,10 +275,13 @@
             device_id_type=MESH,
         ).wait_recv()
 
+    def fill_own(out, source, pair, size, s, w):
+        for t in range(EARLY):
+            out[s][w * SLOTS + t] = source[s][jnp.minimum(code(pair[w], t), size - 1)]
+
     def send_own(out, into, send, recv, source, pair, size, s):
         for w in range(2):
-            for t in range(EARLY):
-                out[s][w * SLOTS + t] = source[s][jnp.minimum(code(pair[w], t), size - 1)]
+            fill_own(out, source, pair, size, s, w)
             copy_of(out, into, send, recv, s, w, 0).start()
 
     def send_on(out, into, send, recv, source, pair, size, s):
@@ -374,8 +377,12 @@
                     device_id_type=MESH,
                 ).start()
 
+    take(0)
+    for w in range(2):
+        fill_own(there_out, own, words[0:2], HELD, 0, w)
     pl.semaphore_wait(barrier, planes)
-    there_own(0)
+    for w in range(2):
+        copy_of(*there, 0, w, 0).start()
     there_own(1)
     there_own(2)
     grad_sum = jnp.zeros((8, LANES), F32)
@@ -579,21 +586,21 @@
     finish(1)
     if zs > 1:
         planes_spread()
+    for s in range(QUARTERS):
+        all_sent(*there, s)
+    for r in range(len(rounds)):
+        exchange_sent(r)
     finish(2)
     if zs > 1:
         totals = planes_end()
+        planes_sent()
     grad_total = jnp.sum(totals[0:8], keepdims=True)
     direction_total = jnp.sum(totals[8:16], keepdims=True)
     scale[...] = jnp.broadcast_to(jnp.sqrt(grad_total / (direction_total + EPSILON)), (8, LANES))
     finish(3)
 
     for s in range(QUARTERS):
-        all_sent(*there, s)
         all_sent(*back, s)
-    for r in range(len(rounds)):
-        exchange_sent(r)
-    if zs > 1:
-        planes_sent()
 
 
 def store(wide, scale, left, right, update, new_left, new_right, narrow, sem):

time: 80.8 us -> 80.6 us (level)
  no operation moved by 1% of the time
where the time goes in v6:
time: 80.6 us; the launch traced here: 80.5 us
  Pallas kernels  79.9 us (99%)
    pallas_call x1, Pallas kernels, local(): pl.pallas_call(functools.partial(kernel, sizes), out_shape=(pltpu.VMEM((h...  76.1 us
    pallas_call x1, Pallas kernels, local(): pl.pallas_call(store, out_shape=(jax.ShapeDtypeStruct((held_rows, LANES),...  3.81 us

profile of v6, /device:TPU:0, one launch (start us, length us, event | category | flops | bytes accessed | tf_op | source)
XLA Modules:
  0.0 80.5 jit_solution(15592582548964435567)
XLA Ops:
  0.6 76.1 %shampoo.1 = (f32[6144,128]{1,0:T(8,128)S(1)}, f32[8,128]{1,0:T(8,128)S(1)}, f32[1024,1024]{1,0:T(8,128)S(1)}, f32[1024,1024]{1,0:T(8,128)S(1)}) custom-call(s32[96]{0:T(128)} %position_in.1, s32[96]{0:T(128)} %owner_in.1, s32[2048]{0:T(1024)} %constant.2.clone.table_in, bf16[6144,128]{1,0:T(8,128)(2,1)} %bitcast.12, f32[1024,1024]{1,0:T(8,128)} %bitcast.8, ...), custom_call_target="tpu_custom_call" | custom-call | tf_op jit(solution)/shard_map/shampoo/pallas_call | solution.py:634
  76.7 3.8 %store.1 = (bf16[6144,128]{1,0:T(8,128)(2,1)}, f32[1024,1024]{1,0:T(8,128)}, f32[1024,1024]{1,0:T(8,128)}) custom-call(f32[6144,128]{1,0:T(8,128)S(1)} %get-tuple-element.10.wide, f32[8,128]{1,0:T(8,128)S(1)} %get-tuple-element.11.scale, f32[1024,1024]{1,0:T(8,128)S(1)} %get-tuple-element.12.left, f32[1024,1024]{1,0:T(8,128)S(1)} %get-tuple-element.13.right), custom_call_target="tpu_custom_call" | custom-call | tf_op jit(solution)/shard_map/store/pallas_call | solution.py:689

commit v7 on v6

--- a/solution.py
+++ b/solution.py
@@ -26,6 +26,7 @@
 EARLIER = B - COLS
 WORDS = 8
 LANES = 128
+STORES = 2
 HUB = 1
 SUBROWS = B // LANES
 F32, BF16 = jnp.float32, jnp.bfloat16
@@ -610,8 +611,8 @@
     ]
     for copy in copies:
         copy.start()
-    rows = PIECE * SUBROWS
-    for k in range(HELD):
+    rows = HELD * PIECE * SUBROWS // STORES
+    for k in range(STORES):
         part = pl.ds(k * rows, rows)
         narrow[part, :] = (scale[0:1, :] * wide[part, :]).astype(BF16)
         copies.append(pltpu.make_async_copy(narrow.at[part], update.at[part], sem.at[2 + k]))
@@ -695,7 +696,7 @@
         ),
         in_specs=[inside] * 4,
         out_specs=(outside,) * 3,
-        scratch_shapes=[pltpu.VMEM((held_rows, LANES), BF16), dma((2 + HELD,))],
+        scratch_shapes=[pltpu.VMEM((held_rows, LANES), BF16), dma((2 + STORES,))],
         compiler_params=pltpu.CompilerParams(vmem_limit_bytes=4 * 1024 * 1024),
         name="store",
     )(*(pltpu.with_memory_space_constraint(value, pltpu.VMEM) for value in results))

time: 80.6 us -> 80.6 us (level)
  no operation moved by 1% of the time
where the time goes in v7:
time: 80.6 us; the launch traced here: 80.5 us
  Pallas kernels  79.9 us (99%)
    pallas_call x1, Pallas kernels, local(): pl.pallas_call(functools.partial(kernel, sizes), out_shape=(pltpu.VMEM((h...  76.1 us
    pallas_call x1, Pallas kernels, local(): pl.pallas_call(store, out_shape=(jax.ShapeDtypeStruct((held_rows, LANES),...  3.79 us

profile of v7, /device:TPU:0, one launch (start us, length us, event | category | flops | bytes accessed | tf_op | source)
XLA Modules:
  0.0 80.5 jit_solution(6633146693275414848)
XLA Ops:
  0.6 76.1 %shampoo.1 = (f32[6144,128]{1,0:T(8,128)S(1)}, f32[8,128]{1,0:T(8,128)S(1)}, f32[1024,1024]{1,0:T(8,128)S(1)}, f32[1024,1024]{1,0:T(8,128)S(1)}) custom-call(s32[96]{0:T(128)} %position_in.1, s32[96]{0:T(128)} %owner_in.1, s32[2048]{0:T(1024)} %constant.2.clone.table_in, bf16[6144,128]{1,0:T(8,128)(2,1)} %bitcast.12, f32[1024,1024]{1,0:T(8,128)} %bitcast.8, ...), custom_call_target="tpu_custom_call" | custom-call | tf_op jit(solution)/shard_map/shampoo/pallas_call | solution.py:635
  76.7 3.8 %store.1 = (bf16[6144,128]{1,0:T(8,128)(2,1)}, f32[1024,1024]{1,0:T(8,128)}, f32[1024,1024]{1,0:T(8,128)}) custom-call(f32[6144,128]{1,0:T(8,128)S(1)} %get-tuple-element.10.wide, f32[8,128]{1,0:T(8,128)S(1)} %get-tuple-element.11.scale, f32[1024,1024]{1,0:T(8,128)S(1)} %get-tuple-element.12.left, f32[1024,1024]{1,0:T(8,128)S(1)} %get-tuple-element.13.right), custom_call_target="tpu_custom_call" | custom-call | tf_op jit(solution)/shard_map/store/pallas_call | solution.py:690
